TPU v7x, 256 devices: a whole 4x4x8 slice. The times are simulated.
256 devices in a mesh: seq: 32 (over y, x, z_lo), resp: 8 (over z_hi, core).
Axes of the slice: x: 4, y: 4, z: 8 (z_hi: 4, z_lo: 2; z = z_hi * 2 + z_lo), core: 2. Of those that a mesh axis runs over, the one named last changes fastest.
Arguments:
- queries: bfloat16 [8, 512, 1024], P('resp', 'seq'), may hold values from -6 to 6
- grad_out: bfloat16 [8, 512, 1024], P('resp', 'seq'), may hold values from -5984 to 5984
- row_lse: bfloat16 [8, 512, 8], P('resp', 'seq'), as said below
- row_delta: bfloat16 [8, 512, 8], P('resp', 'seq'), may hold values from -59904 to 59904
- prefix_keys: bfloat16 [65536, 128], P('seq'), may hold values from -6 to 6
- prefix_values: bfloat16 [65536, 128], P('seq'), may hold values from -6 to 6
- resp_len: int32 [8], P('resp'), may hold values from 128 to 512, as said below
- visible: int32 [8], P('resp'), may hold values from 32768 to 65536, as said below
Outputs:
- grad_queries: bfloat16 [8, 512, 1024], P('resp', 'seq')
- grad_keys: bfloat16 [65536, 128], P(('seq', 'resp'))
- grad_values: bfloat16 [65536, 128], P(('seq', 'resp'))
Inputs may be any that keep to these rules, and one draw needn't show every extreme that they name: `row_lse`: each value lies between log(65536) - 0.05 and log(65536) + 3. `resp_len`: some response has exactly 512 live positions. `visible`: some response sees the whole prompt.
All inputs are finite; a program needn't handle non-finite values.
Results may differ from a plain program's by a relative error of at most 0.0059.
Values may be sent and summed in bfloat16 or wider, within the bound.
A program may use at most 64 MiB of HBM per device.

v0:
```python
import jax
import jax.numpy as jnp
from jax import lax
from jax.sharding import PartitionSpec as P

HD = 128
HEADS = 8


def attend_block(q_rows, do_rows, lse_rows, delta_rows, prefix_keys, prefix_values, row_ok, key_ok):
    count = q_rows.shape[0]
    q_three = q_rows.reshape(count, HEADS, HD)
    do_three = do_rows.reshape(count, HEADS, HD)
    scores = jnp.einsum(
        "rhd,kd->hrk", q_three, prefix_keys, preferred_element_type=jnp.float32
    ) * HD ** (-0.5)
    allowed = row_ok[None, :, None] & key_ok[None, None, :]
    probs = jnp.where(allowed, jnp.exp(scores - lse_rows.astype(jnp.float32).T[:, :, None]), 0.0)
    probs_b = probs.astype(jnp.bfloat16)
    grad_v = jnp.einsum("hrk,rhd->kd", probs_b, do_three, preferred_element_type=jnp.float32)
    grad_probs = jnp.einsum(
        "rhd,kd->hrk", do_three, prefix_values, preferred_element_type=jnp.float32
    )
    grad_scores = (probs * (grad_probs - delta_rows.astype(jnp.float32).T[:, :, None])).astype(
        jnp.bfloat16
    )
    grad_k = jnp.einsum("hrk,rhd->kd", grad_scores, q_three, preferred_element_type=jnp.float32)
    grad_q = jnp.einsum("hrk,kd->rhd", grad_scores, prefix_keys, preferred_element_type=jnp.float32)
    return (grad_q.reshape(count, HEADS * HD), grad_k, grad_v)


def on_device(queries, grad_out, row_lse, row_delta, prefix_keys, prefix_values, resp_len, visible):
    score_scale = HD ** (-0.5)
    key_count = prefix_keys.shape[0]
    width = queries.shape[2]
    seq_index = lax.axis_index("seq")
    length = resp_len[0]
    seen = visible[0]
    key_ok = seq_index * key_count + jnp.arange(key_count, dtype=jnp.int32) < seen
    zero_keys = jnp.zeros((key_count, HD), jnp.float32)

    def terms(q_rows, do_rows, lse_rows, delta_rows, first_row):
        count = q_rows.shape[0]
        row_ok = first_row + jnp.arange(count, dtype=jnp.int32) < length
        return attend_block(
            q_rows, do_rows, lse_rows, delta_rows, prefix_keys, prefix_values, row_ok, key_ok
        )

    gathered = (
        lax.all_gather(queries, "seq", axis=1, tiled=True),
        lax.all_gather(grad_out, "seq", axis=1, tiled=True),
        lax.all_gather(row_lse, "seq", axis=1, tiled=True),
        lax.all_gather(row_delta, "seq", axis=1, tiled=True),
    )
    total_rows = gathered[0].shape[1]
    block_rows = min(64, total_rows)
    block_count = total_rows // block_rows
    stacks = tuple(
        (member[0].reshape(block_count, block_rows, member.shape[2]) for member in gathered)
    )
    firsts = jnp.arange(block_count, dtype=jnp.int32) * block_rows

    def scan_step(carry, item):
        part_q, part_k, part_v = terms(item[0], item[1], item[2], item[3], item[4])
        return ((carry[0] + part_k, carry[1] + part_v), part_q)

    (grad_k, grad_v), query_blocks = lax.scan(scan_step, (zero_keys, zero_keys), stacks + (firsts,))
    query_sum = lax.psum_scatter(
        query_blocks.reshape(1, total_rows, width), "seq", scatter_dimension=1, tiled=True
    )
    key_grads = (
        lax.psum_scatter(grad_k, "resp", scatter_dimension=0, tiled=True),
        lax.psum_scatter(grad_v, "resp", scatter_dimension=0, tiled=True),
    )
    grad_queries = (query_sum * score_scale).astype(jnp.bfloat16)
    grad_keys = (key_grads[0] * score_scale).astype(jnp.bfloat16)
    grad_values = key_grads[1].astype(jnp.bfloat16)
    return (grad_queries, grad_keys, grad_values)


def solution(mesh):
    in_specs = (
        P("resp", "seq", None),
        P("resp", "seq", None),
        P("resp", "seq", None),
        P("resp", "seq", None),
        P("seq", None),
        P("seq", None),
        P("resp"),
        P("resp"),
    )
    out_specs = (P("resp", "seq", None), P(("seq", "resp"), None), P(("seq", "resp"), None))
    return jax.shard_map(
        on_device, mesh=mesh, in_specs=in_specs, out_specs=out_specs, check_vma=False
    )
```

profile of v0, /device:TPU:32, one launch (start us, length us, event | category | flops | bytes accessed | tf_op | source)
XLA Modules:
  0.0 663.1 jit_solution(13001470289645976733)
XLA Ops:
  8.7 0.8 copy.28
  9.5 0.8 copy.30
  10.3 79.5 %all_gather.15 = bf16[1,512,8]{2,0,1:T(2,128)(2,1)S(1)} all-gather(bf16[1,16,8]{2,0,1:T(2,128)(2,1)S(1)} %copy.30), channel_id=1, replica_groups=mesh['seq'=32,'resp'=8] {'seq'}, dimensions={1}, use_global_device_ids=true | all-gather | bytes 8448 | tf_op jit(solution)/shard_map/all_gather | solution.py:53
  89.7 82.1 %all_gather.13 = bf16[1,512,8]{2,0,1:T(2,128)(2,1)S(1)} all-gather(bf16[1,16,8]{2,0,1:T(2,128)(2,1)S(1)} %copy.28), channel_id=1, replica_groups=mesh['seq'=32,'resp'=8] {'seq'}, dimensions={1}, use_global_device_ids=true | all-gather | bytes 8448 | tf_op jit(solution)/shard_map/all_gather | solution.py:52
  171.9 150.2 %all-gather.5.cloned.1.call-done = bf16[1,512,1024]{2,1,0:T(8,128)(2,1)} async-done(((bf16[1,16,1024]{2,1,0:T(8,128)(2,1)}), bf16[1,512,1024]{2,1,0:T(8,128)(2,1)}) %all-gather.5.cloned.1.call-update) | async-done | bytes 1048592 | tf_op jit(solution)/shard_map/all_gather | solution.py:51
  322.0 90.3 %while.15 = (s32[]{:T(128)}, f32[2048,128]{1,0:T(8,128)S(1)}, f32[2048,128]{1,0:T(8,128)S(1)}, f32[8,64,1024]{2,1,0:T(8,128)}, s32[8]{0:T(128)S(1)}, /*index=5*/...) while((s32[]{:T(128)}, f32[2048,128]{1,0:T(8,128)S(1)}, ...), condition=%wide.region_1.2_spmd.clone, body=%wide.region_0.1_spmd.clone.sunk | while | flops 1350702208 | bytes 31996296 | solution.py:67
  322.6 1.3 add_compare_fusion.5
  324.7 1.0 dynamic-slice_bitcast_fusion.3
  325.8 2.3 fusion.42
  328.1 1.3 fusion.45
  329.5 0.7 fusion.43
  331.2 1.3 fusion.44
  333.9 1.3 add_compare_fusion.5
  336.0 1.0 dynamic-slice_bitcast_fusion.3
  337.0 2.3 fusion.42
  339.4 1.3 fusion.45
  340.7 0.7 fusion.43
  342.5 1.3 fusion.44
  345.2 1.3 add_compare_fusion.5
  347.3 1.0 dynamic-slice_bitcast_fusion.3
  348.3 2.3 fusion.42
  350.7 1.3 fusion.45
  352.0 0.7 fusion.43
  353.8 1.3 fusion.44
  356.4 1.3 add_compare_fusion.5
  358.6 1.0 dynamic-slice_bitcast_fusion.3
  359.6 2.3 fusion.42
  362.0 1.3 fusion.45
  363.3 0.7 fusion.43
  365.0 1.3 fusion.44
  366.4 0.7 constant_dynamic-update-slice_fusion.2
  367.7 1.3 add_compare_fusion.5
  369.8 1.0 dynamic-slice_bitcast_fusion.3
  370.9 2.3 fusion.42
  373.2 1.3 fusion.45
  374.6 0.7 fusion.43
  376.3 1.3 fusion.44
  377.7 0.7 constant_dynamic-update-slice_fusion.2
  379.0 1.3 add_compare_fusion.5
  381.1 1.0 dynamic-slice_bitcast_fusion.3
  382.2 2.3 fusion.42
  384.5 1.3 fusion.45
  385.9 0.7 fusion.43
  387.6 1.3 fusion.44
  390.3 1.3 add_compare_fusion.5
  392.4 1.0 dynamic-slice_bitcast_fusion.3
  393.5 2.3 fusion.42
  395.8 1.3 fusion.45
  397.1 0.8 fusion.43
  398.9 1.3 fusion.44
  401.6 1.3 add_compare_fusion.5
  403.7 1.0 dynamic-slice_bitcast_fusion.3
  404.7 2.3 fusion.42
  407.1 1.3 fusion.45
  408.4 0.7 fusion.43
  410.2 1.3 fusion.44
  411.5 0.7 constant_dynamic-update-slice_fusion.2
  412.3 1.0 copy-done.2
  414.5 36.7 %reduce-scatter.8.cloned.1.call-done = f32[256,128]{1,0:T(8,128)} async-done(((f32[2048,128]{1,0:T(8,128)}), f32[256,128]{1,0:T(8,128)}) %reduce-scatter.8.cloned.1.call-update) | async-done | bytes 131088 | tf_op jit(solution)/shard_map/reduce_scatter | solution.py:73
  451.1 1.5 convert_element_type.25
  452.7 38.2 %reduce-scatter.6.cloned.1.call-done = f32[256,128]{1,0:T(8,128)} async-done(((f32[2048,128]{1,0:T(8,128)}), f32[256,128]{1,0:T(8,128)}) %reduce-scatter.6.cloned.1.call-update) | async-done | bytes 131088 | tf_op jit(solution)/shard_map/reduce_scatter | solution.py:72
  490.9 1.5 multiply_convert_fusion
  492.4 162.7 %reduce-scatter.4.cloned.1.call-done = f32[1,16,1024]{2,1,0:T(8,128)} async-done(((f32[1,512,1024]{2,1,0:T(8,128)}), f32[1,16,1024]{2,1,0:T(8,128)}) %reduce-scatter.4.cloned.1.call-update) | async-done | bytes 65552 | tf_op jit(solution)/shard_map/reduce_scatter | solution.py:68
  655.1 1.5 multiply_convert_fusion.1
  (121 shorter events, 26.0 us)
Async XLA Ops:
  7.2 164.7 %all-gather.3.cloned.1.call-start = ((), (), s32[]{:S(2)}) async-start(), calls=%async_computation.3 | async-start | bytes 1081344 | tf_op jit(solution)/shard_map/all_gather | solution.py:50
  7.9 314.1 %all-gather.5.cloned.1.call-start = ((), (), s32[]{:S(2)}) async-start(), calls=%async_computation.4 | async-start | bytes 1081344 | tf_op jit(solution)/shard_map/all_gather | solution.py:51
  8.6 442.5 %reduce-scatter.8.cloned.1.call-start = ((), (), s32[]{:S(2)}) async-start(), calls=%async_computation.7 | async-start | bytes 1179648 | tf_op jit(solution)/shard_map/reduce_scatter | solution.py:73
  328.1 1.3 copy-start.1
  329.5 1.0 copy-start
  339.4 1.3 copy-start.1
  340.7 1.0 copy-start
  350.7 1.3 copy-start.1
  352.0 1.0 copy-start
  361.9 1.3 copy-start.1
  363.3 1.0 copy-start
  373.2 1.3 copy-start.1
  374.6 1.0 copy-start
  384.5 1.3 copy-start.1
  385.9 1.0 copy-start
  395.8 1.3 copy-start.1
  397.1 1.0 copy-start
  407.1 1.3 copy-start.1
  408.4 1.0 copy-start
  412.3 1.0 copy-start.2
  412.3 1.3 copy-start.3
  413.3 77.6 %reduce-scatter.6.cloned.1.call-start = ((), (), s32[]{:S(2)}) async-start(), calls=%async_computation.6 | async-start | bytes 1179648 | tf_op jit(solution)/shard_map/reduce_scatter | solution.py:72
  413.9 241.3 %reduce-scatter.4.cloned.1.call-start = ((), (), s32[]{:S(2)}) async-start(), calls=%async_computation.5 | async-start | bytes 2162688 | tf_op jit(solution)/shard_map/reduce_scatter | solution.py:68
Sparse Core Ops, SparseCore 0:
  9.8 156.7 all-gather.2
  168.4 153.6 all-gather.4
  413.4 37.6 reduce-scatter.7
  453.5 37.2 reduce-scatter.5
  493.2 161.8 reduce-scatter.3
where the time goes:
time: 669 us; the launch traced here: 663 us
  waiting for transfers between devices  390 us (58%)
  blocking collectives  162 us (24%)
  matrix products  51.1 us (8%)
  local copies, waits for them, and re-layouts  24.3 us (4%)
  other arithmetic  21.3 us (3%)
  between operations  13.8 us (2%)
    reduce_scatter x1, waiting for transfers between devices, on_device(): lax.psum_scatter(query_blocks.reshape(1, total_rows, width), 'seq', scatt...  163 us
    all_gather x1, waiting for transfers between devices, on_device(): lax.all_gather(grad_out, 'seq', axis=1, tiled=True)  150 us
    all_gather x1, blocking collectives, on_device(): lax.all_gather(row_lse, 'seq', axis=1, tiled=True)  82.1 us
    all_gather x1, blocking collectives, on_device(): lax.all_gather(row_delta, 'seq', axis=1, tiled=True)  79.5 us
    reduce_scatter x1, waiting for transfers between devices, on_device(): lax.psum_scatter(grad_k, 'resp', scatter_dimension=0, tiled=True)  38.2 us
    reduce_scatter x1, waiting for transfers between devices, on_device(): lax.psum_scatter(grad_v, 'resp', scatter_dimension=0, tiled=True)  36.7 us
    dot_general x8, matrix products, attend_block(): jnp.einsum('rhd,kd->hrk', q_three, prefix_keys, preferred_element_type=jn...  18.6 us
  transfers between devices with their start and end apart: 5, of which 4 were waited for; matrix products, arithmetic and copies ran while one was open for 1% of the time, Pallas kernels for 0%

commit v1 on v0

v1 whole, which is shorter than its diff:
```python
import jax
import jax.numpy as jnp
from jax import lax
from jax.experimental import pallas as pl
from jax.experimental.pallas import tpu as pltpu
from jax.sharding import PartitionSpec as P

HD = 128
HEADS = 8
ROWS = 16
KEYS = 2048
TILE = 512
SLOT = ROWS * HEADS
LOG2E = 1.4426950408889634
SCALE = HD ** -0.5
MESH = pl.DeviceIdType.MESH
f32, bf16 = jnp.float32, jnp.bfloat16

PHASE_A = (((0, 0),), ((0, 1), (0, 3)), ((1, 0), (3, 0), (0, 2)), ((1, 1), (1, 3), (3, 1), (3, 3)))
PHASE_B = (((2, 1), (2, 3), (1, 2), (3, 2)), ((2, 0), (2, 2)))
KEY_ORDER = (2, 1, 3, 0)


def dot(a, b, ca, cb):
    return lax.dot_general(a, b, (((ca,), (cb,)), ((), ())), preferred_element_type=f32)


def kernel(q_in, do_in, lse_in, delta_in, k_in, v_in, len_in, vis_in, oq, ok, ov,
           gq, gd, km, kt, vm, dk, dv, dq, sq, rq, ps, pr, zs, zr,
           s_gather, r_z, r_gq, r_gd, s_dq, r_dq, s_pair, r_pair, s_zs, r_zs):
    seq, resp = lax.axis_index("seq"), lax.axis_index("resp")
    y, x, zl = seq // 8, (seq // 2) % 4, seq % 2
    zh, core = resp // 2, resp % 2

    def seq_peer(dy, dx, dz):
        return ((((y + dy) % 4) * 4 + (x + dx) % 4) * 2 + (zl + dz) % 2, resp)

    def resp_peer(dz, dc):
        return (seq, ((zh + dz) % 4) * 2 + (core + dc) % 2)

    barrier = pltpu.get_barrier_semaphore()
    peers = [seq_peer(dy, dx, dz) for dy in range(4) for dx in range(4) for dz in range(2) if (dy, dx, dz) != (0, 0, 0)]
    peers += [resp_peer(0, 1), resp_peer(1, 0), resp_peer(2, 0), resp_peer(3, 0)]
    for peer in peers:
        pl.semaphore_signal(barrier, inc=1, device_id=peer, device_id_type=MESH)

    live = seq * ROWS + lax.broadcasted_iota(jnp.int32, (ROWS, HD), 0) < len_in[0]
    for h in range(HEADS):
        cols = slice(h * HD, (h + 1) * HD)
        rows = slice(h * ROWS, (h + 1) * ROWS)
        gq[0, rows, :] = jnp.where(live, q_in[:, cols].astype(f32), 0.0).astype(bf16)
        gd[0, rows, :] = jnp.where(live, do_in[:, cols].astype(f32), 0.0).astype(bf16)
    lane = lax.broadcasted_iota(jnp.int32, (ROWS, SLOT), 1)
    spread = jnp.where(lane % ROWS == lax.broadcasted_iota(jnp.int32, (ROWS, SLOT), 0), 1.0, 0.0).astype(bf16)
    head_lane = lax.broadcasted_iota(jnp.int32, (HEADS, SLOT), 1)
    own_head = head_lane // ROWS == lax.broadcasted_iota(jnp.int32, (HEADS, SLOT), 0)
    live_lane = seq * ROWS + head_lane % ROWS < len_in[0]
    lse_row = jnp.sum(jnp.where(own_head, dot(lse_in[...], spread, 1, 0), 0.0), axis=0, keepdims=True)
    delta_row = jnp.sum(jnp.where(own_head & live_lane, dot(delta_in[...], spread, 1, 0), 0.0), axis=0, keepdims=True)
    which = lax.broadcasted_iota(jnp.int32, (ROWS, SLOT), 0)
    gq[0, SLOT:SLOT + ROWS, :] = jnp.where(which == 0, lse_row, jnp.where(which == 1, delta_row, 0.0)).astype(bf16)

    pl.semaphore_wait(barrier, len(peers))

    started = []

    def send(src, dst, send_sem, recv_sem, peer):
        copy = pltpu.make_async_remote_copy(
            src_ref=src, dst_ref=dst, send_sem=send_sem, recv_sem=recv_sem, device_id=peer, device_id_type=MESH)
        copy.start()
        started.append(copy)

    def arrived(dst, recv_sem):
        pltpu.make_async_remote_copy(
            src_ref=dst, dst_ref=dst, send_sem=s_gather.at[0], recv_sem=recv_sem,
            device_id=seq_peer(0, 0, 1), device_id_type=MESH).wait_recv()

    def pair(ref, dy, dx):
        return ref.at[pl.ds(2 * (dy * 4 + dx), 2)]

    count = [0]

    def gather_sem():
        count[0] += 1
        return s_gather.at[count[0] - 1]

    send(gq.at[0], gq.at[1], gather_sem(), r_z.at[0], seq_peer(0, 0, 1))
    send(gd.at[0], gd.at[1], gather_sem(), r_z.at[1], seq_peer(0, 0, 1))
    arrived(gq.at[1], r_z.at[0])
    arrived(gd.at[1], r_z.at[1])
    for step in (1, 3, 2):
        back = (4 - step) % 4
        send(pair(gq, 0, 0), pair(gq, 0, back), gather_sem(), r_gq.at[back], seq_peer(0, step, 0))
        send(pair(gd, 0, 0), pair(gd, back, 0), gather_sem(), r_gd.at[back * 4], seq_peer(step, 0, 0))
        send(pair(gd, 0, 0), pair(gd, 0, back), gather_sem(), r_gd.at[back], seq_peer(0, step, 0))
        send(pair(gq, 0, 0), pair(gq, back, 0), gather_sem(), r_gq.at[back * 4], seq_peer(step, 0, 0))

    def pass_on(step):
        arrived(pair(gq, 0, step), r_gq.at[step])
        for dy in (1, 3, 2):
            back = (4 - dy) % 4
            send(pair(gq, 0, step), pair(gq, back, step), gather_sem(), r_gq.at[back * 4 + step], seq_peer(dy, 0, 0))
        arrived(pair(gd, step, 0), r_gd.at[step * 4])
        for dx in (1, 3, 2):
            back = (4 - dx) % 4
            send(pair(gd, step, 0), pair(gd, step, back), gather_sem(), r_gd.at[step * 4 + back], seq_peer(0, dx, 0))

    def need(pairs):
        for dy, dx in pairs:
            if (dy, dx) == (0, 0):
                continue
            if dy:
                arrived(pair(gq, dy, dx), r_gq.at[dy * 4 + dx])
            if dx:
                arrived(pair(gd, dy, dx), r_gd.at[dy * 4 + dx])

    half = TILE // 2

    def block_start(dz, dc):
        return pl.multiple_of((((zh + dz) % 4) * 2 + (core + dc) % 2) * half, half)

    def seen_rows(dz, dc):
        first = seq * KEYS + block_start(dz, dc)
        return first + lax.broadcasted_iota(jnp.int32, (half, HD), 0) < vis_in[0]

    for dz in range(4):
        for dc in range(2):
            src = pl.ds(block_start(dz, dc), half)
            dst = slice((dz * 2 + dc) * half, (dz * 2 + dc + 1) * half)
            block = jnp.where(seen_rows(dz, dc), k_in[src, :].astype(f32), 0.0)
            km[dst, :] = block.astype(bf16)
            kt[:, dst] = block.T.astype(bf16)
            vm[dst, :] = v_in[src, :]

    def attend(pairs, at, k0, first_q, first_k):
        own = slice(at, at + 256 * len(pairs))
        qb = jnp.concatenate([gq[2 * (a * 4 + b):2 * (a * 4 + b) + 2, 0:SLOT, :].reshape(256, HD) for a, b in pairs], axis=0)
        dob = jnp.concatenate([gd[2 * (a * 4 + b):2 * (a * 4 + b) + 2].reshape(256, HD) for a, b in pairs], axis=0)
        slots = [2 * (a * 4 + b) + c for a, b in pairs for c in range(2)]
        stats = [gq[s, SLOT:SLOT + ROWS, :].astype(f32) for s in slots]
        lse = jnp.concatenate([s[0:1, :] for s in stats], axis=1) * LOG2E
        delta = jnp.concatenate([s[1:2, :] for s in stats], axis=1)
        keys = pl.ds(k0, TILE)
        kb, vb = km[keys, :], vm[keys, :]
        probs = jnp.exp2(dot(kb, qb, 1, 1) * (SCALE * LOG2E) - lse)
        grads = (probs * (dot(vb, dob, 1, 1) - delta)).astype(bf16)
        probs = probs.astype(bf16)
        part_q = dot(kt[:, keys], grads, 1, 0)
        part_v = dot(probs, dob, 1, 0)
        part_k = dot(grads, qb, 1, 0)
        if first_q:
            dq[:, own] = part_q
        else:
            dq[:, own] += part_q
        if first_k:
            dk[keys, :] = part_k
            dv[keys, :] = part_v
        else:
            dk[keys, :] += part_k
            dv[keys, :] += part_v

    def send_queries(pairs, at):
        for n, (dy, dx) in enumerate(pairs):
            for dz in range(2):
                s = 2 * (dy * 4 + dx) + dz
                lanes = slice(at + (2 * n + dz) * SLOT, at + (2 * n + dz + 1) * SLOT)
                if s == 0:
                    rq[0] = dq[:, lanes].astype(bf16)
                else:
                    sq[s] = dq[:, lanes].astype(bf16)
                    send(sq.at[s], rq.at[s], s_dq.at[s], r_dq.at[s], seq_peer(dy, dx, dz))

    for n, pairs in enumerate(PHASE_A):
        need(pairs)
        width = 256 * len(pairs)
        dq[:, 0:width] = jnp.zeros((HD, width), f32)

        def one(i, carry, pairs=pairs, n=n):
            attend(pairs, 0, pl.multiple_of(i * TILE, TILE), False, n == 0)
            return carry

        lax.fori_loop(0, KEYS // TILE, one, 0)
        send_queries(pairs, 0)
        if n == 0:
            pass_on(1)
            pass_on(3)
        if n == 1:
            pass_on(2)

    def finish_keys(dz):
        for dc in (1, 0):
            rows = slice((dz * 2 + dc) * half, (dz * 2 + dc + 1) * half)
            seen = seen_rows(dz, dc)
            for n, total in enumerate((dk, dv)):
                part = jnp.where(seen, total[rows, :], 0.0)
                if dc:
                    ps[dz, n * half:(n + 1) * half, :] = part.astype(bf16)
                else:
                    total[rows, :] = part
            if dc:
                send(ps.at[dz], pr.at[dz], s_pair.at[dz], r_pair.at[dz], resp_peer(0, 1))

    def pass_keys(dz):
        arrived(pr.at[dz], r_pair.at[dz])
        rows = slice(dz * 2 * half, (dz * 2 + 1) * half)
        for n, total in enumerate((dk, dv)):
            zs[dz, n * half:(n + 1) * half, :] = (
                total[rows, :] + pr[dz, n * half:(n + 1) * half, :].astype(f32)).astype(bf16)
        send(zs.at[dz], zr.at[dz], s_zs.at[dz], r_zs.at[dz], resp_peer(dz, 0))

    for pairs in PHASE_B:
        need(pairs)
    offsets = [0]
    for pairs in PHASE_B:
        offsets.append(offsets[-1] + 256 * len(pairs))

    for i, dz in enumerate(KEY_ORDER):
        for n, pairs in enumerate(PHASE_B):
            attend(pairs, offsets[n], dz * TILE, i == 0, False)
            if i == 3:
                send_queries(pairs, offsets[n])
        finish_keys(dz)
        if i:
            pass_keys(KEY_ORDER[i - 1])

    arrived(pr.at[0], r_pair.at[0])
    totals = [dk[0:half, :] + pr[0, 0:half, :].astype(f32), dv[0:half, :] + pr[0, half:TILE, :].astype(f32)]
    for dz in (2, 1, 3):
        arrived(zr.at[dz], r_zs.at[dz])
        totals = [t + zr[dz, n * half:(n + 1) * half, :].astype(f32) for n, t in enumerate(totals)]
    ok[...] = (totals[0] * SCALE).astype(bf16)
    ov[...] = totals[1].astype(bf16)

    total = rq[0].astype(f32)
    for s in range(1, 32):
        arrived(rq.at[s], r_dq.at[s])
        total += rq[s].astype(f32)
    total = (total.T * SCALE).astype(bf16)
    for h in range(HEADS):
        oq[:, h * HD:(h + 1) * HD] = total[h * ROWS:(h + 1) * ROWS, :]
    for copy in started:
        copy.wait_send()


def on_device(queries, grad_out, row_lse, row_delta, prefix_keys, prefix_values, resp_len, visible):
    vmem, smem = pl.BlockSpec(memory_space=pltpu.VMEM), pl.BlockSpec(memory_space=pltpu.SMEM)
    dma = pltpu.SemaphoreType.DMA
    owned = KEYS // 8
    grad_queries, grad_keys, grad_values = pl.pallas_call(
        kernel,
        out_shape=(
            jax.ShapeDtypeStruct((ROWS, HEADS * HD), bf16),
            jax.ShapeDtypeStruct((owned, HD), bf16),
            jax.ShapeDtypeStruct((owned, HD), bf16),
        ),
        in_specs=[vmem] * 6 + [smem] * 2,
        out_specs=(vmem, vmem, vmem),
        scratch_shapes=[
            pltpu.VMEM((32, SLOT + ROWS, HD), bf16),
            pltpu.VMEM((32, SLOT, HD), bf16),
            pltpu.VMEM((KEYS, HD), bf16),
            pltpu.VMEM((HD, KEYS), bf16),
            pltpu.VMEM((KEYS, HD), bf16),
            pltpu.VMEM((KEYS, HD), f32),
            pltpu.VMEM((KEYS, HD), f32),
            pltpu.VMEM((HD, 2048), f32),
            pltpu.VMEM((32, HD, SLOT), bf16),
            pltpu.VMEM((32, HD, SLOT), bf16),
            pltpu.VMEM((4, TILE, HD), bf16),
            pltpu.VMEM((4, TILE, HD), bf16),
            pltpu.VMEM((4, TILE, HD), bf16),
            pltpu.VMEM((4, TILE, HD), bf16),
            dma((32,)), dma((2,)), dma((16,)), dma((16,)),
            dma((32,)), dma((32,)), dma((4,)), dma((4,)), dma((4,)), dma((4,)),
        ],
        compiler_params=pltpu.CompilerParams(
            collective_id=0, has_side_effects=True, vmem_limit_bytes=48 * 1024 * 1024),
    )(queries[0], grad_out[0], row_lse[0].T, row_delta[0].T, prefix_keys, prefix_values, resp_len, visible)
    return grad_queries[None], grad_keys, grad_values


def solution(mesh):
    in_specs = (
        P("resp", "seq", None),
        P("resp", "seq", None),
        P("resp", "seq", None),
        P("resp", "seq", None),
        P("seq", None),
        P("seq", None),
        P("resp"),
        P("resp"),
    )
    out_specs = (P("resp", "seq", None), P(("seq", "resp"), None), P(("seq", "resp"), None))
    return jax.shard_map(
        on_device, mesh=mesh, in_specs=in_specs, out_specs=out_specs, check_vma=False
    )
```

time: 669 us -> 67.8 us (0.10)
  waiting for transfers between devices: 390 us -> 0 us
  blocking collectives: 162 us -> 0 us
  Pallas kernels: 0 us -> 59.3 us
  matrix products: 51.1 us -> 0 us
  other arithmetic: 21.3 us -> 0 us
  local copies, waits for them, and re-layouts: 24.3 us -> 6.15 us
  between operations: 13.8 us -> 1.95 us
    reduce_scatter x3 -> x0, waiting for transfers between devices: 238 us -> none  [the longest x1 163 us: on_device(): lax.psum_scatter(query_blocks.reshape(1, total_rows, width), 'seq', scatt...]
    all_gather x2 -> x0, blocking collectives: 162 us -> none  [the longest x1 82.1 us: on_device(): lax.all_gather(row_lse, 'seq', axis=1, tiled=True)]
    all_gather x2 -> x0, waiting for transfers between devices: 150 us -> none  [the longest x1 150 us: on_device(): lax.all_gather(grad_out, 'seq', axis=1, tiled=True)]
    pallas_call x0 -> x1, Pallas kernels: none -> 59.3 us  [on_device(): pl.pallas_call(kernel, out_shape=(jax.ShapeDtypeStruct((ROWS, HEADS * HD)...]
    dot_general x40 -> x0, matrix products: 51.1 us -> none  [the longest x8 18.6 us: attend_block(): jnp.einsum('rhd,kd->hrk', q_three, prefix_keys, preferred_element_type=jn...]
    lt x16 -> x0, other arithmetic: 15.6 us -> none  [the longest x8 10.4 us: terms(): row_ok = first_row + jnp.arange(count, dtype=jnp.int32) < length]
    while x56 -> x0, local copies, waits for them, and re-layouts: 10.6 us -> none
  transfers between devices with their start and end apart: 5 -> 0, of which waited for: 4 -> 0; matrix products, arithmetic and copies ran while one was open for 1% -> 0% of each run, Pallas kernels for 0% -> 0%
where the time goes in v1:
time: 67.8 us; the launch traced here: 67.4 us
  Pallas kernels  59.3 us (87%)
  local copies, waits for them, and re-layouts  6.15 us (9%)
  between operations  1.95 us (3%)
    pallas_call x1, Pallas kernels, on_device(): pl.pallas_call(kernel, out_shape=(jax.ShapeDtypeStruct((ROWS, HEADS * HD)...  59.3 us
    unnamed x15, local copies, waits for them, and re-layouts  6.15 us

profile of v1, /device:TPU:32, one launch (start us, length us, event | category | flops | bytes accessed | tf_op | source)
XLA Modules:
  0.0 67.4 jit_solution(7235896145208751830)
XLA Ops:
  1.9 0.0 copy-start.5
  1.9 0.0 copy-start.4
  1.9 0.7 copy-done.5
  2.6 0.0 copy-done.4
  2.6 0.0 copy-start
  2.6 1.0 %copy-done = bf16[2048,128]{1,0:T(8,128)(2,1)S(1)} copy-done((bf16[2048,128]{1,0:T(8,128)(2,1)S(1)}, bf16[2048,128]{1,0:T(8,128)(2,1)}, u32[]{:S(2)}) %copy-start) | copy-done | bytes 524312
  3.7 0.0 copy-start.1
  3.7 1.0 %copy-done.1 = bf16[2048,128]{1,0:T(8,128)(2,1)S(1)} copy-done((bf16[2048,128]{1,0:T(8,128)(2,1)S(1)}, bf16[2048,128]{1,0:T(8,128)(2,1)}, u32[]{:S(2)}) %copy-start.1) | copy-done | bytes 524312
  4.7 0.0 copy-start.2
  4.7 0.8 %copy-done.2 = bf16[1,16,1024]{2,1,0:T(8,128)(2,1)S(1)} copy-done((bf16[1,16,1024]{2,1,0:T(8,128)(2,1)S(1)}, bf16[1,16,1024]{2,1,0:T(8,128)(2,1)}, u32[]{:S(2)}) %copy-start.2) | copy-done | bytes 32792
  5.5 0.0 copy-start.3
  5.5 0.8 %copy-done.3 = bf16[1,16,1024]{2,1,0:T(8,128)(2,1)S(1)} copy-done((bf16[1,16,1024]{2,1,0:T(8,128)(2,1)S(1)}, bf16[1,16,1024]{2,1,0:T(8,128)(2,1)}, u32[]{:S(2)}) %copy-start.3) | copy-done | bytes 32792
  6.2 59.3 %shard_map.103 = (bf16[16,1024]{1,0:T(8,128)(2,1)S(1)}, bf16[256,128]{1,0:T(8,128)(2,1)S(1)}, bf16[256,128]{1,0:T(8,128)(2,1)S(1)}) custom-call(bf16[16,1024]{1,0:T(8,128)(2,1)S(1)} %bitcast.9, bf16[16,1024]{1,0:T(8,128)(2,1)S(1)} %bitcast.10, bf16[8,16]{1,0:T(8,128)(2,1)S(1)} %bitcast.12, bf16[8,16]{1,0:T(8,128)(2,1)S(1)} %bitcast.13, ...), custom_call_target="tpu_custom_call" | custom-call | tf_op jit(solution)/shard_map/pallas_call | solution.py:249
  65.5 0.6 copy.16
  66.2 0.6 copy.17
  66.8 0.6 copy.18
Async XLA Ops:
  1.9 0.7 %copy-start.5 = (bf16[1,16,8]{1,2,0:T(8,128)(2,1)S(1)}, bf16[1,16,8]{1,2,0:T(8,128)(2,1)}, u32[]{:S(2)}) copy-start(bf16[1,16,8]{1,2,0:T(8,128)(2,1)} %param.11) | copy-start | bytes 772
  1.9 0.7 %copy-start.4 = (bf16[1,16,8]{1,2,0:T(8,128)(2,1)S(1)}, bf16[1,16,8]{1,2,0:T(8,128)(2,1)}, u32[]{:S(2)}) copy-start(bf16[1,16,8]{1,2,0:T(8,128)(2,1)} %param.10) | copy-start | bytes 772
  2.6 1.0 %copy-start = (bf16[2048,128]{1,0:T(8,128)(2,1)S(1)}, bf16[2048,128]{1,0:T(8,128)(2,1)}, u32[]{:S(2)}) copy-start(bf16[2048,128]{1,0:T(8,128)(2,1)} %k_in.1) | copy-start | bytes 1572868
  3.7 1.0 %copy-start.1 = (bf16[2048,128]{1,0:T(8,128)(2,1)S(1)}, bf16[2048,128]{1,0:T(8,128)(2,1)}, u32[]{:S(2)}) copy-start(bf16[2048,128]{1,0:T(8,128)(2,1)} %v_in.1) | copy-start | bytes 1572868
  4.7 0.8 %copy-start.2 = (bf16[1,16,1024]{2,1,0:T(8,128)(2,1)S(1)}, bf16[1,16,1024]{2,1,0:T(8,128)(2,1)}, u32[]{:S(2)}) copy-start(bf16[1,16,1024]{2,1,0:T(8,128)(2,1)} %param.8) | copy-start | bytes 98308
  5.5 0.8 %copy-start.3 = (bf16[1,16,1024]{2,1,0:T(8,128)(2,1)S(1)}, bf16[1,16,1024]{2,1,0:T(8,128)(2,1)}, u32[]{:S(2)}) copy-start(bf16[1,16,1024]{2,1,0:T(8,128)(2,1)} %param.9) | copy-start | bytes 98308

commit v2 on v1

v2 whole, which is shorter than its diff:
```python
import jax
import jax.numpy as jnp
from jax import lax
from jax.experimental import pallas as pl
from jax.experimental.pallas import tpu as pltpu
from jax.sharding import PartitionSpec as P

HD = 128
HEADS = 8
ROWS = 16
KEYS = 2048
TILE = 512
SLOT = ROWS * HEADS
DO = SLOT + ROWS
LOG2E = 1.4426950408889634
SCALE = HD ** -0.5
MESH = pl.DeviceIdType.MESH
f32, bf16 = jnp.float32, jnp.bfloat16

ALONG = (1, 3, 2)
FAR = tuple((dy, dx) for dy in ALONG for dx in ALONG)
OWN = ((0, 0, 0),)
NEAR_0 = ((0, 1, 0), (0, 3, 0), (1, 0, 0), (3, 0, 0))
TWO_0 = ((0, 2, 0), (2, 0, 0))
PARTNER = ((0, 0, 1),)
LINE_1 = tuple((dy, dx, 1) for dy, dx, _ in NEAR_0 + TWO_0)
FAR_0 = tuple((dy, dx, 0) for dy, dx in FAR)
FAR_1 = tuple((dy, dx, 1) for dy, dx in FAR)
ORDER = OWN + NEAR_0 + TWO_0 + PARTNER + LINE_1 + FAR_0 + FAR_1
QUARTER = TILE // 4
PIECES = (
    ((2, 0, 0, 256), (2, 1, 0, 256)),
    ((1, 0, 0, 128), (3, 0, 0, 128), (1, 1, 0, 128), (3, 1, 0, 128)),
    ((1, 0, 128, 128), (3, 0, 128, 128), (1, 1, 128, 128), (3, 1, 128, 128)),
    ((0, 0, 0, 256), (0, 1, 0, 256)),
)


def dot(a, b, ca, cb):
    return lax.dot_general(a, b, (((ca,), (cb,)), ((), ())), preferred_element_type=f32)


def kernel(q_in, do_in, lse_in, delta_in, k_in, v_in, len_in, vis_in, oq, ok, ov,
           q_own, do_own, lse_own, delta_own, k_own, vm, rows_all, km, kt, dk, dv, dq, sq, r1, s2, r2, s3, r3,
           ps, pr, zs, zr, s_in, s_gather, r_slot, r_fq, r_fd, s_dq, r_dq, s_pair, r_pair, s_zs, r_zs):
    seq, resp = lax.axis_index("seq"), lax.axis_index("resp")
    y, x, zl = seq // 8, (seq // 2) % 4, seq % 2
    zh, core = resp // 2, resp % 2

    def seq_peer(dy, dx, dz):
        return ((((y + dy) % 4) * 4 + (x + dx) % 4) * 2 + (zl + dz) % 2, resp)

    def resp_peer(dz, dc):
        return (seq, ((zh + dz) % 4) * 2 + (core + dc) % 2)

    loads = [pltpu.make_async_copy(src, dst, s_in.at[n]) for n, (src, dst) in enumerate(
        ((q_in, q_own), (do_in, do_own), (lse_in, lse_own), (delta_in, delta_own), (k_in, k_own)))]
    for load in loads:
        load.start()

    barrier = pltpu.get_barrier_semaphore()
    peers = [seq_peer(0, 0, 1)] + [seq_peer(d, 0, 0) for d in (1, 2, 3)] + [seq_peer(0, d, 0) for d in (1, 2, 3)]
    peers += [resp_peer(0, 1), resp_peer(1, 0), resp_peer(2, 0), resp_peer(3, 0)]
    for peer in peers:
        pl.semaphore_signal(barrier, inc=1, device_id=peer, device_id_type=MESH)

    half = TILE // 2
    pieces = []
    for n, step in enumerate(PIECES):
        at = n * TILE
        for dz, dc, first, count in step:
            start = pl.multiple_of((((zh + dz) % 4) * 2 + (core + dc) % 2) * half + first, QUARTER)
            pieces.append((n, start, slice(at, at + count), count))
            at += count
    for n, start, rows, count in pieces:
        loads.append(pltpu.make_async_copy(v_in.at[pl.ds(start, count)], vm.at[rows], s_in.at[len(loads)]))
        loads[-1].start()

    for load in loads[:4]:
        load.wait()
    live = seq * ROWS + lax.broadcasted_iota(jnp.int32, (ROWS, HD), 0) < len_in[0]
    for h in range(HEADS):
        cols = slice(h * HD, (h + 1) * HD)
        rows_all[0, h * ROWS:(h + 1) * ROWS, :] = jnp.where(live, q_own[:, cols].astype(f32), 0.0).astype(bf16)
        rows_all[0, DO + h * ROWS:DO + (h + 1) * ROWS, :] = jnp.where(live, do_own[:, cols].astype(f32), 0.0).astype(bf16)
    lane = lax.broadcasted_iota(jnp.int32, (ROWS, SLOT), 1)
    spread = jnp.where(lane % ROWS == lax.broadcasted_iota(jnp.int32, (ROWS, SLOT), 0), 1.0, 0.0).astype(bf16)
    head_lane = lax.broadcasted_iota(jnp.int32, (HEADS, SLOT), 1)
    own_head = head_lane // ROWS == lax.broadcasted_iota(jnp.int32, (HEADS, SLOT), 0)
    live_lane = seq * ROWS + head_lane % ROWS < len_in[0]
    lse_row = jnp.sum(jnp.where(own_head, dot(lse_own[...], spread, 1, 0), 0.0), axis=0, keepdims=True)
    delta_row = jnp.sum(jnp.where(own_head & live_lane, dot(delta_own[...], spread, 1, 0), 0.0), axis=0, keepdims=True)
    which = lax.broadcasted_iota(jnp.int32, (ROWS, SLOT), 0)
    rows_all[0, SLOT:DO, :] = jnp.where(which == 0, lse_row, jnp.where(which == 1, delta_row, 0.0)).astype(bf16)

    pl.semaphore_wait(barrier, len(peers))

    started = []

    def send(src, dst, send_sem, recv_sem, peer):
        copy = pltpu.make_async_remote_copy(
            src_ref=src, dst_ref=dst, send_sem=send_sem, recv_sem=recv_sem, device_id=peer, device_id_type=MESH)
        copy.start()
        started.append(copy)

    waited = set()

    def arrived(dst, recv_sem, name):
        if name in waited:
            return
        waited.add(name)
        pltpu.make_async_remote_copy(
            src_ref=dst, dst_ref=dst, send_sem=s_gather.at[0], recv_sem=recv_sem,
            device_id=seq_peer(0, 0, 1), device_id_type=MESH).wait_recv()

    sends = [0]

    def gather_sem():
        sends[0] += 1
        return s_gather.at[sends[0] - 1]

    def place(dy, dx):
        return (dy % 4) * 4 + dx % 4

    def slot(dy, dx, dz):
        return 2 * place(dy, dx) + dz

    def q_part(n):
        return rows_all.at[n, 0:DO]

    def do_part(n):
        return rows_all.at[n, DO:DO + SLOT]

    def along_lines(dz):
        for step in ALONG:
            for dy, dx in ((0, step), (step, 0)):
                at = slot(-dy, -dx, dz)
                send(rows_all.at[dz], rows_all.at[at], gather_sem(), r_slot.at[at], seq_peer(dy, dx, 0))

    def get(slots):
        for dy, dx, dz in slots:
            at = slot(dy, dx, dz)
            if dy and dx:
                arrived(q_part(at), r_fq.at[at], (at, "q"))
                arrived(do_part(at), r_fd.at[at], (at, "do"))
            elif at:
                arrived(rows_all.at[at], r_slot.at[at], at)

    def pass_on(slots):
        get(slots)
        for step in ALONG:
            for dy, dx, dz in slots:
                at = slot(dy, dx, dz)
                if dx:
                    to = slot(-step, dx, dz)
                    send(q_part(at), q_part(to), gather_sem(), r_fq.at[to], seq_peer(step, 0, 0))
                else:
                    to = slot(dy, -step, dz)
                    send(do_part(at), do_part(to), gather_sem(), r_fd.at[to], seq_peer(0, step, 0))

    send(rows_all.at[0], rows_all.at[1], gather_sem(), r_slot.at[1], seq_peer(0, 0, 1))
    along_lines(0)

    def seen_rows(start, count):
        return seq * KEYS + start + lax.broadcasted_iota(jnp.int32, (count, HD), 0) < vis_in[0]

    loads[4].wait()
    for n, start, rows, count in pieces:
        block = jnp.where(seen_rows(start, count), k_own[pl.ds(start, count), :].astype(f32), 0.0)
        km[rows, :] = block.astype(bf16)
        kt[:, rows] = block.T.astype(bf16)
    for load in loads[5:]:
        load.wait()

    def lanes(slots):
        at = ORDER.index(slots[0])
        return slice(at * SLOT, (at + len(slots)) * SLOT)

    def attend(slots, k0, tile, first_q, first_k):
        own = lanes(slots)
        places = [slot(*name) for name in slots]
        qb = jnp.concatenate([rows_all[p, 0:SLOT, :] for p in places], axis=0)
        dob = jnp.concatenate([rows_all[p, DO:DO + SLOT, :] for p in places], axis=0)
        stats = [rows_all[p, SLOT:DO, :].astype(f32) for p in places]
        lse = jnp.concatenate([s[0:1, :] for s in stats], axis=1) * LOG2E
        delta = jnp.concatenate([s[1:2, :] for s in stats], axis=1)
        keys = pl.ds(k0, tile)
        kb, vb = km[keys, :], vm[keys, :]
        probs = jnp.exp2(dot(kb, qb, 1, 1) * (SCALE * LOG2E) - lse)
        grads = (probs * (dot(vb, dob, 1, 1) - delta)).astype(bf16)
        probs = probs.astype(bf16)
        part_q = dot(kt[:, keys], grads, 1, 0)
        part_v = dot(probs, dob, 1, 0)
        part_k = dot(grads, qb, 1, 0)
        if first_q:
            dq[:, own] = part_q
        else:
            dq[:, own] += part_q
        if first_k:
            dk[keys, :] = part_k
            dv[keys, :] = part_v
        else:
            dk[keys, :] += part_k
            dv[keys, :] += part_v

    def source(c, n, step):
        return (c * 4 + n) * 3 + step - 1

    def send_queries(slots):
        for dy, dx, dz in slots:
            step, other = (dy, dx) if dz else (dx, dy)
            if step == 0:
                continue
            n = slot(dy, dx, dz)
            to = source(dz, other, 4 - step)
            sq[n] = dq[:, lanes(((dy, dx, dz),))].astype(bf16)
            send(sq.at[n], r1.at[to], s_dq.at[n], r_dq.at[to], seq_peer(dy, 0, 0) if dz else seq_peer(0, dx, 0))

    def line_sum(c, n):
        total = dq[:, lanes((((0, n, 1) if c else (n, 0, 0)),))]
        for step in (1, 3, 2):
            at = source(c, n, step)
            arrived(r1.at[at], r_dq.at[at], ("r1", at))
            total += r1[at].astype(f32)
        return total

    def send_line(c, n):
        at = c * 3 + n - 1
        to = c * 3 + (4 - n) - 1
        s2[at] = line_sum(c, n).astype(bf16)
        send(s2.at[at], r2.at[to], s_dq.at[32 + at], r_dq.at[24 + to], seq_peer(n, 0, 0) if c == 0 else seq_peer(0, n, 0))

    def own_sum(c):
        total = line_sum(c, 0)
        for n in (1, 2, 3):
            at = c * 3 + n - 1
            arrived(r2.at[at], r_dq.at[24 + at], ("r2", at))
            total += r2[at].astype(f32)
        return total

    def finish_keys(n):
        for m, start, rows, count in pieces:
            if m != n:
                continue
            seen = seen_rows(start, count)
            for which, total in enumerate((dk, dv)):
                part = jnp.where(seen, total[rows, :], 0.0)
                at = rows.start - n * TILE - half
                if at < 0:
                    total[rows, :] = part
                else:
                    ps[n, which * half + at:which * half + at + count, :] = part.astype(bf16)
        send(ps.at[n], pr.at[n], s_pair.at[n], r_pair.at[n], resp_peer(0, 1))

    def pair_sums(n):
        arrived(pr.at[n], r_pair.at[n], ("pair", n))
        return [total[n * TILE:n * TILE + half, :] + pr[n, which * half:(which + 1) * half, :].astype(f32)
                for which, total in enumerate((dk, dv))]

    def pass_keys(n):
        sums = pair_sums(n)
        for m, (dz, _, _, count) in enumerate(PIECES[n][:len(PIECES[n]) // 2]):
            at = 0 if n == 0 else TILE * n + m * half
            for which in range(2):
                zs[at + which * count:at + (which + 1) * count, :] = sums[which][m * count:(m + 1) * count, :].astype(bf16)
            whole, sem = pl.ds(at, 2 * count), 2 * n + m
            send(zs.at[whole], zr.at[whole], s_zs.at[sem], r_zs.at[sem], resp_peer(dz, 0))

    def from_others(first, count):
        n = 1 + first // QUARTER
        sums = [part[first:first + count, :] for part in own_keys]
        for at, size, skip, sem in ((0, half, first, 0), (TILE * n, count, 0, 2 * n), (TILE * n + half, count, 0, 2 * n + 1)):
            arrived(zr.at[pl.ds(at, 2 * size)], r_zs.at[sem], ("zr", at))
            sums = [t + zr[at + which * size + skip:at + which * size + skip + count, :].astype(f32) for which, t in enumerate(sums)]
        ok[first:first + count, :] = (sums[0] * SCALE).astype(bf16)
        ov[first:first + count, :] = sums[1].astype(bf16)

    for n in range(2):
        attend(OWN, n * 1024, 1024, n == 0, True)
    get(PARTNER)
    along_lines(1)
    pass_on(NEAR_0)
    attend(NEAR_0, 0, 1024, True, False)
    pass_on(TWO_0)
    attend(NEAR_0, 1024, TILE, False, False)
    attend(TWO_0 + PARTNER, 0, 1024, True, False)
    pass_on(LINE_1[:4])
    attend(TWO_0 + PARTNER, 1024, TILE, False, False)
    pass_on(LINE_1[4:])
    for n in range(3):
        attend(LINE_1, n * TILE, TILE, n == 0, False)
    get(FAR_0)
    for n in range(3):
        attend(FAR_0, n * TILE, TILE, n == 0, False)
    get(FAR_1)
    for n in range(3):
        attend(FAR_1, n * TILE, TILE, n == 0, False)
        if n:
            pass_keys(n - 1)
        finish_keys(n)
    attend(FAR_1, 3 * TILE, TILE, False, False)
    pass_keys(2)
    send_queries(FAR_1)
    attend(FAR_0, 3 * TILE, TILE, False, False)
    send_queries(FAR_0)
    attend(PARTNER + LINE_1, 3 * TILE, TILE, False, False)
    send_queries(LINE_1)
    for n in (2, 1, 3):
        send_line(1, n)
    attend(NEAR_0 + TWO_0, 3 * TILE, TILE, False, False)
    send_queries(NEAR_0 + TWO_0)
    finish_keys(3)
    for n in (2, 1, 3):
        send_line(0, n)
    s3[...] = own_sum(1)
    send(s3, r3, s_dq.at[38], r_dq.at[30], seq_peer(0, 0, 1))
    own_keys = pair_sums(3)
    for n in range(2):
        from_others(n * QUARTER, QUARTER)
    total = own_sum(0)
    arrived(r3, r_dq.at[30], "r3")
    total = ((total + r3[...]).T * SCALE).astype(bf16)
    for h in range(HEADS):
        oq[:, h * HD:(h + 1) * HD] = total[h * ROWS:(h + 1) * ROWS, :]
    for copy in started:
        copy.wait_send()


def on_device(queries, grad_out, row_lse, row_delta, prefix_keys, prefix_values, resp_len, visible):
    vmem, smem, hbm = (pl.BlockSpec(memory_space=space) for space in (pltpu.VMEM, pltpu.SMEM, pltpu.HBM))
    dma = pltpu.SemaphoreType.DMA
    owned = KEYS // 8
    grad_queries, grad_keys, grad_values = pl.pallas_call(
        kernel,
        out_shape=(
            jax.ShapeDtypeStruct((ROWS, HEADS * HD), bf16),
            jax.ShapeDtypeStruct((owned, HD), bf16),
            jax.ShapeDtypeStruct((owned, HD), bf16),
        ),
        in_specs=[hbm] * 6 + [smem] * 2,
        out_specs=(vmem, vmem, vmem),
        scratch_shapes=[
            pltpu.VMEM((ROWS, HEADS * HD), bf16),
            pltpu.VMEM((ROWS, HEADS * HD), bf16),
            pltpu.VMEM((HEADS, ROWS), bf16),
            pltpu.VMEM((HEADS, ROWS), bf16),
            pltpu.VMEM((KEYS, HD), bf16),
            pltpu.VMEM((KEYS, HD), bf16),
            pltpu.VMEM((32, DO + SLOT, HD), bf16),
            pltpu.VMEM((KEYS, HD), bf16),
            pltpu.VMEM((HD, KEYS), bf16),
            pltpu.VMEM((KEYS, HD), f32),
            pltpu.VMEM((KEYS, HD), f32),
            pltpu.VMEM((HD, 32 * SLOT), f32),
            pltpu.VMEM((32, HD, SLOT), bf16),
            pltpu.VMEM((24, HD, SLOT), bf16),
            pltpu.VMEM((6, HD, SLOT), bf16),
            pltpu.VMEM((6, HD, SLOT), bf16),
            pltpu.VMEM((HD, SLOT), f32),
            pltpu.VMEM((HD, SLOT), f32),
            pltpu.VMEM((4, TILE, HD), bf16),
            pltpu.VMEM((4, TILE, HD), bf16),
            pltpu.VMEM((3 * TILE, HD), bf16),
            pltpu.VMEM((3 * TILE, HD), bf16),
            dma((17,)), dma((49,)), dma((32,)), dma((32,)), dma((32,)),
            dma((39,)), dma((31,)), dma((4,)), dma((4,)), dma((6,)), dma((6,)),
        ],
        compiler_params=pltpu.CompilerParams(
            collective_id=0, has_side_effects=True, vmem_limit_bytes=64 * 1024 * 1024),
    )(queries[0], grad_out[0], row_lse[0].T, row_delta[0].T, prefix_keys, prefix_values, resp_len, visible)
    return grad_queries[None], grad_keys, grad_values


def solution(mesh):
    in_specs = (
        P("resp", "seq", None),
        P("resp", "seq", None),
        P("resp", "seq", None),
        P("resp", "seq", None),
        P("seq", None),
        P("seq", None),
        P("resp"),
        P("resp"),
    )
    out_specs = (P("resp", "seq", None), P(("seq", "resp"), None), P(("seq", "resp"), None))
    return jax.shard_map(
        on_device, mesh=mesh, in_specs=in_specs, out_specs=out_specs, check_vma=False
    )
```

time: 67.8 us -> 57.1 us (0.84)
  Pallas kernels: 59.3 us -> 52.1 us
  local copies, waits for them, and re-layouts: 6.15 us -> 2.9 us
    pallas_call x1, Pallas kernels: 59.3 us -> 52.1 us  [on_device(): pl.pallas_call(kernel, out_shape=(jax.ShapeDtypeStruct((ROWS, HEADS * HD)...]
    unnamed x15 -> x7, local copies, waits for them, and re-layouts: 6.15 us -> 2.9 us
where the time goes in v2:
time: 57.1 us; the launch traced here: 56.9 us
  Pallas kernels  52.1 us (91%)
  local copies, waits for them, and re-layouts  2.9 us (5%)
  between operations  1.94 us (3%)
    pallas_call x1, Pallas kernels, on_device(): pl.pallas_call(kernel, out_shape=(jax.ShapeDtypeStruct((ROWS, HEADS * HD)...  52.1 us
    unnamed x7, local copies, waits for them, and re-layouts  2.9 us

profile of v2, /device:TPU:32, one launch (start us, length us, event | category | flops | bytes accessed | tf_op | source)
XLA Modules:
  0.0 56.9 jit_solution(4746652053563282388)
XLA Ops:
  1.9 52.1 %shard_map.103 = (bf16[16,1024]{1,0:T(8,128)(2,1)}, bf16[256,128]{1,0:T(8,128)(2,1)}, bf16[256,128]{1,0:T(8,128)(2,1)}) custom-call(bf16[16,1024]{1,0:T(8,128)(2,1)} %bitcast.9, bf16[16,1024]{1,0:T(8,128)(2,1)} %bitcast.10, bf16[8,16]{1,0:T(8,128)(2,1)} %bitcast.12, bf16[8,16]{1,0:T(8,128)(2,1)} %bitcast.13, bf16[2048,128]{1,0:T(8,128)(2,1)} %k_in.1, ...), custom_call_target="tpu_custom_call" | custom-call | tf_op jit(solution)/shard_map/pallas_call | solution.py:333
  54.0 0.0 copy-start.1
  54.0 1.4 %copy.16 = bf16[1,16,1024]{2,1,0:T(8,128)(2,1)} copy(bf16[1,16,1024]{2,1,0:T(8,128)(2,1)} %bitcast.11) | data formatting | bytes 65536
  55.4 0.0 copy-done.1
  55.4 0.0 copy-start
  55.5 0.6 %copy.17 = bf16[256,128]{1,0:T(8,128)(2,1)} copy(bf16[256,128]{1,0:T(8,128)(2,1)S(1)} %copy-done.1) | data formatting | bytes 131072
  56.1 0.2 copy-done
  56.3 0.6 %copy.18 = bf16[256,128]{1,0:T(8,128)(2,1)} copy(bf16[256,128]{1,0:T(8,128)(2,1)S(1)} %copy-done) | data formatting | bytes 131072
Async XLA Ops:
  54.0 1.4 %copy-start.1 = (bf16[256,128]{1,0:T(8,128)(2,1)S(1)}, bf16[256,128]{1,0:T(8,128)(2,1)}, u32[]{:S(2)}) copy-start(bf16[256,128]{1,0:T(8,128)(2,1)} %get-tuple-element.13) | copy-start | bytes 196612
  55.4 0.9 %copy-start = (bf16[256,128]{1,0:T(8,128)(2,1)S(1)}, bf16[256,128]{1,0:T(8,128)(2,1)}, u32[]{:S(2)}) copy-start(bf16[256,128]{1,0:T(8,128)(2,1)} %get-tuple-element.14) | copy-start | bytes 196612

commit v3 on v2

v3 whole, which is shorter than its diff:
```python
import jax
import jax.numpy as jnp
from jax import lax
from jax.experimental import pallas as pl
from jax.experimental.pallas import tpu as pltpu
from jax.sharding import PartitionSpec as P

HD = 128
HEADS = 8
ROWS = 16
KEYS = 2048
TILE = 512
SLOT = ROWS * HEADS
DO = SLOT + ROWS
LOG2E = 1.4426950408889634
SCALE = HD ** -0.5
MESH = pl.DeviceIdType.MESH
f32, bf16 = jnp.float32, jnp.bfloat16

ALONG = (1, 3, 2)
FAR = tuple((dy, dx) for dy in ALONG for dx in ALONG)
OWN = ((0, 0, 0),)
NEAR_0 = ((0, 1, 0), (0, 3, 0), (1, 0, 0), (3, 0, 0))
TWO_0 = ((0, 2, 0), (2, 0, 0))
PARTNER = ((0, 0, 1),)
LINE_1 = tuple((dy, dx, 1) for dy, dx, _ in NEAR_0 + TWO_0)
FAR_0 = tuple((dy, dx, 0) for dy, dx in FAR)
FAR_1 = tuple((dy, dx, 1) for dy, dx in FAR)
ORDER = OWN + TWO_0 + NEAR_0 + PARTNER + LINE_1 + FAR_0 + FAR_1
QUARTER = TILE // 4
PIECES = (
    ((2, 0, 0, 256), (2, 1, 0, 256)),
    ((1, 0, 0, 128), (3, 0, 0, 128), (1, 1, 0, 128), (3, 1, 0, 128)),
    ((1, 0, 128, 128), (3, 0, 128, 128), (1, 1, 128, 128), (3, 1, 128, 128)),
    ((0, 0, 0, 256), (0, 1, 0, 256)),
)


def dot(a, b, ca, cb):
    return lax.dot_general(a, b, (((ca,), (cb,)), ((), ())), preferred_element_type=f32)


def kernel(q_in, do_in, lse_in, delta_in, k_in, v_in, len_in, vis_in, oq, ok, ov,
           q_own, do_own, lse_own, delta_own, k_own, vm, rows_all, km, kt, dk, dv, dq, sq, r1, s2, r2, s3, r3,
           ps, pr, zs, zr, s_in, s_gather, r_line, r_fq, r_fd, s_dq, r_dq, s_pair, r_pair, s_zs, r_zs, near_sem, far_sem):
    seq, resp = lax.axis_index("seq"), lax.axis_index("resp")
    y, x, zl = seq // 8, (seq // 2) % 4, seq % 2
    zh, core = resp // 2, resp % 2

    def seq_peer(dy, dx, dz):
        return ((((y + dy) % 4) * 4 + (x + dx) % 4) * 2 + (zl + dz) % 2, resp)

    def resp_peer(dz, dc):
        return (seq, ((zh + dz) % 4) * 2 + (core + dc) % 2)

    loads = [pltpu.make_async_copy(src, dst, s_in.at[n]) for n, (src, dst) in enumerate(
        ((q_in, q_own), (do_in, do_own), (lse_in, lse_own), (delta_in, delta_own), (k_in, k_own)))]
    for load in loads:
        load.start()

    barrier = pltpu.get_barrier_semaphore()
    z_side = (seq_peer(0, 0, 1)[0], ((zh + 2 * zl + 3) % 4) * 2 + core)
    neighbours = [seq_peer(0, 0, 1), z_side] + [seq_peer(dy, dx, 0) for dy, dx in ((0, 1), (0, 3), (1, 0), (3, 0))]
    for peer in neighbours + [resp_peer(0, 1)]:
        pl.semaphore_signal(barrier, inc=1, device_id=peer, device_id_type=MESH)

    half = TILE // 2
    pieces = []
    for n, step in enumerate(PIECES):
        at = n * TILE
        for dz, dc, first, count in step:
            start = pl.multiple_of((((zh + dz) % 4) * 2 + (core + dc) % 2) * half + first, QUARTER)
            pieces.append((n, start, slice(at, at + count), count))
            at += count
    for n, start, rows, count in pieces:
        loads.append(pltpu.make_async_copy(v_in.at[pl.ds(start, count)], vm.at[rows], s_in.at[len(loads)]))
        loads[-1].start()

    for load in loads[:4]:
        load.wait()
    live = seq * ROWS + lax.broadcasted_iota(jnp.int32, (ROWS, HD), 0) < len_in[0]
    for h in range(HEADS):
        cols = slice(h * HD, (h + 1) * HD)
        rows_all[0, 0, 0, h * ROWS:(h + 1) * ROWS, :] = jnp.where(live, q_own[:, cols].astype(f32), 0.0).astype(bf16)
        rows_all[0, 0, 0, DO + h * ROWS:DO + (h + 1) * ROWS, :] = jnp.where(live, do_own[:, cols].astype(f32), 0.0).astype(bf16)
    lane = lax.broadcasted_iota(jnp.int32, (ROWS, SLOT), 1)
    spread = jnp.where(lane % ROWS == lax.broadcasted_iota(jnp.int32, (ROWS, SLOT), 0), 1.0, 0.0).astype(bf16)
    head_lane = lax.broadcasted_iota(jnp.int32, (HEADS, SLOT), 1)
    own_head = head_lane // ROWS == lax.broadcasted_iota(jnp.int32, (HEADS, SLOT), 0)
    live_lane = seq * ROWS + head_lane % ROWS < len_in[0]
    lse_row = jnp.sum(jnp.where(own_head, dot(lse_own[...], spread, 1, 0), 0.0), axis=0, keepdims=True)
    delta_row = jnp.sum(jnp.where(own_head & live_lane, dot(delta_own[...], spread, 1, 0), 0.0), axis=0, keepdims=True)
    which = lax.broadcasted_iota(jnp.int32, (ROWS, SLOT), 0)
    rows_all[0, 0, 0, SLOT:DO, :] = jnp.where(which == 0, lse_row, jnp.where(which == 1, delta_row, 0.0)).astype(bf16)

    pl.semaphore_wait(barrier, len(neighbours) + 1)
    for peer in neighbours:
        pl.semaphore_signal(near_sem, inc=1, device_id=peer, device_id_type=MESH)

    started = []

    def send(src, dst, send_sem, recv_sem, peer):
        copy = pltpu.make_async_remote_copy(
            src_ref=src, dst_ref=dst, send_sem=send_sem, recv_sem=recv_sem, device_id=peer, device_id_type=MESH)
        copy.start()
        started.append(copy)

    waited = set()

    def arrived(dst, recv_sem, name):
        if name in waited:
            return
        waited.add(name)
        pltpu.make_async_remote_copy(
            src_ref=dst, dst_ref=dst, send_sem=s_gather.at[0], recv_sem=recv_sem,
            device_id=seq_peer(0, 0, 1), device_id_type=MESH).wait_recv()

    sends = [0]

    def gather_sem():
        sends[0] += 1
        return s_gather.at[sends[0] - 1]

    def rows_of(dy, dx, dz):
        return rows_all.at[dz, dy % 4, dx % 4]

    def along_lines(dz, steps=ALONG):
        for step in steps:
            for n, (dy, dx) in enumerate(((0, step), (step, 0))):
                send(rows_of(0, 0, dz), rows_of(-dy, -dx, dz), gather_sem(), r_line.at[dz * 6 + n * 3 + 3 - step], seq_peer(dy, dx, 0))

    def get(slots):
        for dy, dx, dz in slots:
            if not dy and not dx:
                arrived(rows_of(0, 0, 1), r_line.at[12], "z")
            elif not dy or not dx:
                sem = dz * 6 + (3 if dy else 0) + dy + dx - 1
                arrived(rows_of(dy, dx, dz), r_line.at[sem], ("line", sem))
            else:
                arrived(queries_from(dz, dy), r_fq.at[dz * 3 + dy - 1], ("q", dz, dy))
                arrived(grads_from(dz, dx), r_fd.at[dz * 3 + dx - 1], ("do", dz, dx))

    def queries_from(dz, dy):
        return rows_all.at[dz, dy % 4, 1:4, 0:DO]

    def grads_from(dz, dx):
        return rows_all.at[dz, 1:4, dx % 4, DO:DO + SLOT]

    def pass_on(dz):
        for step in ALONG:
            sem = dz * 3 + 3 - step
            send(queries_from(dz, 0), queries_from(dz, -step), gather_sem(), r_fq.at[sem], seq_peer(step, 0, 0))
            send(grads_from(dz, 0), grads_from(dz, -step), gather_sem(), r_fd.at[sem], seq_peer(0, step, 0))

    send(rows_of(0, 0, 0), rows_of(0, 0, 1), gather_sem(), r_line.at[12], seq_peer(0, 0, 1))
    along_lines(0, (1, 3))

    def meet_far():
        pl.semaphore_wait(near_sem, len(neighbours))
        for dz in (1, 3):
            pl.semaphore_signal(far_sem, inc=1, device_id=resp_peer(dz, 0), device_id_type=MESH)

    def seen_rows(start, count):
        return seq * KEYS + start + lax.broadcasted_iota(jnp.int32, (count, HD), 0) < vis_in[0]

    loads[4].wait()
    for n, start, rows, count in pieces:
        block = jnp.where(seen_rows(start, count), k_own[pl.ds(start, count), :].astype(f32), 0.0)
        km[rows, :] = block.astype(bf16)
        kt[:, rows] = block.T.astype(bf16)
    meet_far()
    along_lines(0, (2,))
    for load in loads[5:]:
        load.wait()

    def lanes(slots):
        at = ORDER.index(slots[0])
        return slice(at * SLOT, (at + len(slots)) * SLOT)

    def attend(slots, k0, tile, first_q, first_k):
        own = lanes(slots)
        qb = jnp.concatenate([rows_all[dz, dy, dx, 0:SLOT, :] for dy, dx, dz in slots], axis=0)
        dob = jnp.concatenate([rows_all[dz, dy, dx, DO:DO + SLOT, :] for dy, dx, dz in slots], axis=0)
        stats = [rows_all[dz, dy, dx, SLOT:DO, :].astype(f32) for dy, dx, dz in slots]
        lse = jnp.concatenate([s[0:1, :] for s in stats], axis=1) * LOG2E
        delta = jnp.concatenate([s[1:2, :] for s in stats], axis=1)
        keys = pl.ds(k0, tile)
        kb, vb = km[keys, :], vm[keys, :]
        probs = jnp.exp2(dot(kb, qb, 1, 1) * (SCALE * LOG2E) - lse)
        grads = (probs * (dot(vb, dob, 1, 1) - delta)).astype(bf16)
        probs = probs.astype(bf16)
        part_q = dot(kt[:, keys], grads, 1, 0)
        part_v = dot(probs, dob, 1, 0)
        part_k = dot(grads, qb, 1, 0)
        if first_q:
            dq[:, own] = part_q
        else:
            dq[:, own] += part_q
        if first_k:
            dk[keys, :] = part_k
            dv[keys, :] = part_v
        else:
            dk[keys, :] += part_k
            dv[keys, :] += part_v

    def send_queries(c, far):
        for step in ALONG:
            for other in ((1, 2, 3) if far else (0,)):
                name = (step, other, 1) if c else (other, step, 0)
                sq[c, step - 1, other] = dq[:, lanes((name,))].astype(bf16)
            rows = slice(1, 4) if far else 0
            sem, to = c * 6 + 3 * far + step - 1, c * 6 + 3 * far + 3 - step
            send(sq.at[c, step - 1, rows], r1.at[c, 3 - step, rows], s_dq.at[sem], r_dq.at[to], seq_peer(step, 0, 0) if c else seq_peer(0, step, 0))

    def line_sum(c, n):
        total = dq[:, lanes((((0, n, 1) if c else (n, 0, 0)),))]
        far = 1 if n else 0
        for step in ALONG:
            rows, sem = (slice(1, 4) if far else 0), c * 6 + 3 * far + step - 1
            arrived(r1.at[c, step - 1, rows], r_dq.at[sem], ("r1", sem))
            total += r1[c, step - 1, n].astype(f32)
        return total

    def send_line(c, n):
        at = c * 3 + n - 1
        to = c * 3 + (4 - n) - 1
        s2[at] = line_sum(c, n).astype(bf16)
        send(s2.at[at], r2.at[to], s_dq.at[12 + at], r_dq.at[12 + to], seq_peer(0, n, 0) if c else seq_peer(n, 0, 0))

    def own_sum(c):
        total = line_sum(c, 0)
        for n in (1, 2, 3):
            at = c * 3 + n - 1
            arrived(r2.at[at], r_dq.at[12 + at], ("r2", at))
            total += r2[at].astype(f32)
        return total

    def finish_keys(n):
        for m, start, rows, count in pieces:
            if m != n:
                continue
            seen = seen_rows(start, count)
            for which, total in enumerate((dk, dv)):
                part = jnp.where(seen, total[rows, :], 0.0)
                at = rows.start - n * TILE - half
                if at < 0:
                    total[rows, :] = part
                else:
                    ps[n, which * half + at:which * half + at + count, :] = part.astype(bf16)
        send(ps.at[n], pr.at[n], s_pair.at[n], r_pair.at[n], resp_peer(0, 1))

    def pair_sums(n):
        arrived(pr.at[n], r_pair.at[n], ("pair", n))
        return [total[n * TILE:n * TILE + half, :] + pr[n, which * half:(which + 1) * half, :].astype(f32)
                for which, total in enumerate((dk, dv))]

    def pass_farthest():
        sums = pair_sums(0)
        for which in range(2):
            for part in range(2):
                at = (part * 2 + which) * QUARTER
                zs[at:at + QUARTER, :] = sums[which][part * QUARTER:(part + 1) * QUARTER, :].astype(bf16)
        for at, count, sem, dz in ((half, QUARTER, 1, 1), (half + QUARTER, QUARTER, 6, 3), (0, half, 0, 2)):
            send(zs.at[pl.ds(at, count)], zr.at[pl.ds(at, count)], s_zs.at[sem], r_zs.at[sem], resp_peer(dz, 0))

    def pass_keys(n):
        sums = pair_sums(n)
        for m in range(2):
            at, sem = TILE * n + m * half, 2 * n + m
            for which in range(2):
                part = sums[which][m * QUARTER:(m + 1) * QUARTER, :]
                if n == 2 and m == which:
                    other = half + m * QUARTER
                    arrived(zr.at[pl.ds(other, QUARTER)], r_zs.at[1 + 5 * m], ("relay", m))
                    part += zr[other:other + QUARTER, :].astype(f32)
                zs[at + which * QUARTER:at + (which + 1) * QUARTER, :] = part.astype(bf16)
            send(zs.at[pl.ds(at, half)], zr.at[pl.ds(at, half)], s_zs.at[sem], r_zs.at[sem], resp_peer(1 + 2 * m, 0))

    def from_others(n):
        rows = slice((n - 1) * QUARTER, n * QUARTER)
        sums = [part[rows, :] for part in own_keys]
        for at, sem in ((TILE * n, 2 * n), (TILE * n + half, 2 * n + 1), (0, 0))[:4 - n]:
            arrived(zr.at[pl.ds(at, half)], r_zs.at[sem], ("zr", at))
            sums = [t + zr[at + which * QUARTER:at + (which + 1) * QUARTER, :].astype(f32) for which, t in enumerate(sums)]
        ok[rows, :] = (sums[0] * SCALE).astype(bf16)
        ov[rows, :] = sums[1].astype(bf16)

    for n in range(2):
        attend(OWN, n * 1024, 1024, n == 0, True)
    get(PARTNER)
    along_lines(1)
    get(NEAR_0)
    attend(NEAR_0 + PARTNER, 0, 1024, True, False)
    get(TWO_0)
    pass_on(0)
    attend(NEAR_0 + PARTNER, 1024, TILE, False, False)
    attend(TWO_0, 0, 1024, True, False)
    attend(TWO_0, 1024, TILE, False, False)
    get(LINE_1)
    pass_on(1)
    for n in range(3):
        attend(LINE_1, n * TILE, TILE, n == 0, False)
    get(FAR_0)
    for n in range(3):
        attend(FAR_0, n * TILE, TILE, n == 0, False)
    get(FAR_1)
    pl.semaphore_wait(far_sem, 2)
    for n in range(3):
        attend(FAR_1, n * TILE, TILE, n == 0, False)
        if n == 1:
            pass_farthest()
        if n == 2:
            pass_keys(1)
        finish_keys(n)
    attend(FAR_1, 3 * TILE, TILE, False, False)
    send_queries(1, 1)
    attend(FAR_0, 3 * TILE, TILE, False, False)
    pass_keys(2)
    send_queries(0, 1)
    attend(PARTNER + LINE_1, 3 * TILE, TILE, False, False)
    send_queries(1, 0)
    attend(TWO_0 + NEAR_0, 3 * TILE, TILE, False, False)
    send_queries(0, 0)
    finish_keys(3)
    for n in ALONG:
        send_line(1, n)
    for n in ALONG:
        send_line(0, n)
    s3[...] = own_sum(1)
    send(s3, r3, s_dq.at[18], r_dq.at[18], seq_peer(0, 0, 1))
    own_keys = pair_sums(3)
    for n in (1, 2):
        from_others(n)
    total = own_sum(0)
    arrived(r3, r_dq.at[18], "r3")
    total = ((total + r3[...]).T * SCALE).astype(bf16)
    for h in range(HEADS):
        oq[:, h * HD:(h + 1) * HD] = total[h * ROWS:(h + 1) * ROWS, :]
    for copy in started:
        copy.wait_send()


def on_device(queries, grad_out, row_lse, row_delta, prefix_keys, prefix_values, resp_len, visible):
    vmem, smem, hbm = (pl.BlockSpec(memory_space=space) for space in (pltpu.VMEM, pltpu.SMEM, pltpu.HBM))
    dma = pltpu.SemaphoreType.DMA
    owned = KEYS // 8
    grad_queries, grad_keys, grad_values = pl.pallas_call(
        kernel,
        out_shape=(
            jax.ShapeDtypeStruct((ROWS, HEADS * HD), bf16),
            jax.ShapeDtypeStruct((owned, HD), bf16),
            jax.ShapeDtypeStruct((owned, HD), bf16),
        ),
        in_specs=[hbm] * 6 + [smem] * 2,
        out_specs=(vmem, vmem, vmem),
        scratch_shapes=[
            pltpu.VMEM((ROWS, HEADS * HD), bf16),
            pltpu.VMEM((ROWS, HEADS * HD), bf16),
            pltpu.VMEM((HEADS, ROWS), bf16),
            pltpu.VMEM((HEADS, ROWS), bf16),
            pltpu.VMEM((KEYS, HD), bf16),
            pltpu.VMEM((KEYS, HD), bf16),
            pltpu.VMEM((2, 4, 4, DO + SLOT, HD), bf16),
            pltpu.VMEM((KEYS, HD), bf16),
            pltpu.VMEM((HD, KEYS), bf16),
            pltpu.VMEM((KEYS, HD), f32),
            pltpu.VMEM((KEYS, HD), f32),
            pltpu.VMEM((HD, 32 * SLOT), f32),
            pltpu.VMEM((2, 3, 4, HD, SLOT), bf16),
            pltpu.VMEM((2, 3, 4, HD, SLOT), bf16),
            pltpu.VMEM((6, HD, SLOT), bf16),
            pltpu.VMEM((6, HD, SLOT), bf16),
            pltpu.VMEM((HD, SLOT), f32),
            pltpu.VMEM((HD, SLOT), f32),
            pltpu.VMEM((4, TILE, HD), bf16),
            pltpu.VMEM((4, TILE, HD), bf16),
            pltpu.VMEM((3 * TILE, HD), bf16),
            pltpu.VMEM((3 * TILE, HD), bf16),
            dma((17,)), dma((25,)), dma((13,)), dma((6,)), dma((6,)),
            dma((19,)), dma((19,)), dma((4,)), dma((4,)), dma((7,)), dma((7,)),
            pltpu.SemaphoreType.REGULAR, pltpu.SemaphoreType.REGULAR,
        ],
        compiler_params=pltpu.CompilerParams(
            collective_id=0, has_side_effects=True, vmem_limit_bytes=64 * 1024 * 1024),
    )(queries[0], grad_out[0], row_lse[0].T, row_delta[0].T, prefix_keys, prefix_values, resp_len, visible)
    return grad_queries[None], grad_keys, grad_values


def solution(mesh):
    in_specs = (
        P("resp", "seq", None),
        P("resp", "seq", None),
        P("resp", "seq", None),
        P("resp", "seq", None),
        P("seq", None),
        P("seq", None),
        P("resp"),
        P("resp"),
    )
    out_specs = (P("resp", "seq", None), P(("seq", "resp"), None), P(("seq", "resp"), None))
    return jax.shard_map(
        on_device, mesh=mesh, in_specs=in_specs, out_specs=out_specs, check_vma=False
    )
```

time: 57.1 us -> 55.1 us (0.965)
  Pallas kernels: 52.1 us -> 50.1 us
    pallas_call x1, Pallas kernels: 52.1 us -> 50.1 us  [on_device(): pl.pallas_call(kernel, out_shape=(jax.ShapeDtypeStruct((ROWS, HEADS * HD)...]
where the time goes in v3:
time: 55.1 us; the launch traced here: 54.9 us
  Pallas kernels  50.1 us (91%)
  local copies, waits for them, and re-layouts  2.9 us (5%)
  between operations  1.94 us (4%)
    pallas_call x1, Pallas kernels, on_device(): pl.pallas_call(kernel, out_shape=(jax.ShapeDtypeStruct((ROWS, HEADS * HD)...  50.1 us
    unnamed x7, local copies, waits for them, and re-layouts  2.9 us

profile of v3, /device:TPU:32, one launch (start us, length us, event | category | flops | bytes accessed | tf_op | source)
XLA Modules:
  0.0 54.9 jit_solution(5710845372590574536)
XLA Ops:
  1.9 50.1 %shard_map.103 = (bf16[16,1024]{1,0:T(8,128)(2,1)}, bf16[256,128]{1,0:T(8,128)(2,1)}, bf16[256,128]{1,0:T(8,128)(2,1)}) custom-call(bf16[16,1024]{1,0:T(8,128)(2,1)} %bitcast.9, bf16[16,1024]{1,0:T(8,128)(2,1)} %bitcast.10, bf16[8,16]{1,0:T(8,128)(2,1)} %bitcast.12, bf16[8,16]{1,0:T(8,128)(2,1)} %bitcast.13, bf16[2048,128]{1,0:T(8,128)(2,1)} %k_in.1, ...), custom_call_target="tpu_custom_call" | custom-call | tf_op jit(solution)/shard_map/pallas_call | solution.py:347
  52.0 0.0 copy-start.1
  52.0 1.4 %copy.16 = bf16[1,16,1024]{2,1,0:T(8,128)(2,1)} copy(bf16[1,16,1024]{2,1,0:T(8,128)(2,1)} %bitcast.11) | data formatting | bytes 65536
  53.4 0.0 copy-done.1
  53.4 0.0 copy-start
  53.4 0.6 %copy.17 = bf16[256,128]{1,0:T(8,128)(2,1)} copy(bf16[256,128]{1,0:T(8,128)(2,1)S(1)} %copy-done.1) | data formatting | bytes 131072
  54.1 0.2 copy-done
  54.3 0.6 %copy.18 = bf16[256,128]{1,0:T(8,128)(2,1)} copy(bf16[256,128]{1,0:T(8,128)(2,1)S(1)} %copy-done) | data formatting | bytes 131072
Async XLA Ops:
  52.0 1.4 %copy-start.1 = (bf16[256,128]{1,0:T(8,128)(2,1)S(1)}, bf16[256,128]{1,0:T(8,128)(2,1)}, u32[]{:S(2)}) copy-start(bf16[256,128]{1,0:T(8,128)(2,1)} %get-tuple-element.13) | copy-start | bytes 196612
  53.4 0.9 %copy-start = (bf16[256,128]{1,0:T(8,128)(2,1)S(1)}, bf16[256,128]{1,0:T(8,128)(2,1)}, u32[]{:S(2)}) copy-start(bf16[256,128]{1,0:T(8,128)(2,1)} %get-tuple-element.14) | copy-start | bytes 196612

commit v4 on v3

--- a/solution.py
+++ b/solution.py
@@ -41,7 +41,7 @@
 
 
 def kernel(q_in, do_in, lse_in, delta_in, k_in, v_in, len_in, vis_in, oq, ok, ov,
-           q_own, do_own, lse_own, delta_own, k_own, vm, rows_all, km, kt, dk, dv, dq, sq, r1, s2, r2, s3, r3,
+           q_own, do_own, k_own, vm, rows_all, km, kt, dk, dv, dq, sq, r1, s2, r2, s3, r3,
            ps, pr, zs, zr, s_in, s_gather, r_line, r_fq, r_fd, s_dq, r_dq, s_pair, r_pair, s_zs, r_zs, near_sem, far_sem):
     seq, resp = lax.axis_index("seq"), lax.axis_index("resp")
     y, x, zl = seq // 8, (seq // 2) % 4, seq % 2
@@ -54,7 +54,7 @@
         return (seq, ((zh + dz) % 4) * 2 + (core + dc) % 2)
 
     loads = [pltpu.make_async_copy(src, dst, s_in.at[n]) for n, (src, dst) in enumerate(
-        ((q_in, q_own), (do_in, do_own), (lse_in, lse_own), (delta_in, delta_own), (k_in, k_own)))]
+        ((q_in, q_own), (do_in, do_own), (k_in, k_own)))]
     for load in loads:
         load.start()
 
@@ -76,7 +76,7 @@
         loads.append(pltpu.make_async_copy(v_in.at[pl.ds(start, count)], vm.at[rows], s_in.at[len(loads)]))
         loads[-1].start()
 
-    for load in loads[:4]:
+    for load in loads[:2]:
         load.wait()
     live = seq * ROWS + lax.broadcasted_iota(jnp.int32, (ROWS, HD), 0) < len_in[0]
     for h in range(HEADS):
@@ -88,8 +88,8 @@
     head_lane = lax.broadcasted_iota(jnp.int32, (HEADS, SLOT), 1)
     own_head = head_lane // ROWS == lax.broadcasted_iota(jnp.int32, (HEADS, SLOT), 0)
     live_lane = seq * ROWS + head_lane % ROWS < len_in[0]
-    lse_row = jnp.sum(jnp.where(own_head, dot(lse_own[...], spread, 1, 0), 0.0), axis=0, keepdims=True)
-    delta_row = jnp.sum(jnp.where(own_head & live_lane, dot(delta_own[...], spread, 1, 0), 0.0), axis=0, keepdims=True)
+    lse_row = jnp.sum(jnp.where(own_head, dot(lse_in[...], spread, 1, 0), 0.0), axis=0, keepdims=True)
+    delta_row = jnp.sum(jnp.where(own_head & live_lane, dot(delta_in[...], spread, 1, 0), 0.0), axis=0, keepdims=True)
     which = lax.broadcasted_iota(jnp.int32, (ROWS, SLOT), 0)
     rows_all[0, 0, 0, SLOT:DO, :] = jnp.where(which == 0, lse_row, jnp.where(which == 1, delta_row, 0.0)).astype(bf16)
 
@@ -163,14 +163,14 @@
     def seen_rows(start, count):
         return seq * KEYS + start + lax.broadcasted_iota(jnp.int32, (count, HD), 0) < vis_in[0]
 
-    loads[4].wait()
+    loads[2].wait()
     for n, start, rows, count in pieces:
         block = jnp.where(seen_rows(start, count), k_own[pl.ds(start, count), :].astype(f32), 0.0)
         km[rows, :] = block.astype(bf16)
         kt[:, rows] = block.T.astype(bf16)
     meet_far()
     along_lines(0, (2,))
-    for load in loads[5:]:
+    for load in loads[3:]:
         load.wait()
 
     def lanes(slots):
@@ -285,14 +285,13 @@
         ok[rows, :] = (sums[0] * SCALE).astype(bf16)
         ov[rows, :] = sums[1].astype(bf16)
 
+    get(PARTNER)
+    along_lines(1)
     for n in range(2):
         attend(OWN, n * 1024, 1024, n == 0, True)
-    get(PARTNER)
-    along_lines(1)
-    get(NEAR_0)
+    get(NEAR_0 + TWO_0)
+    pass_on(0)
     attend(NEAR_0 + PARTNER, 0, 1024, True, False)
-    get(TWO_0)
-    pass_on(0)
     attend(NEAR_0 + PARTNER, 1024, TILE, False, False)
     attend(TWO_0, 0, 1024, True, False)
     attend(TWO_0, 1024, TILE, False, False)
@@ -326,16 +325,16 @@
         send_line(1, n)
     for n in ALONG:
         send_line(0, n)
-    s3[...] = own_sum(1)
+    s3[...] = own_sum(1).astype(bf16)
     send(s3, r3, s_dq.at[18], r_dq.at[18], seq_peer(0, 0, 1))
     own_keys = pair_sums(3)
     for n in (1, 2):
         from_others(n)
     total = own_sum(0)
     arrived(r3, r_dq.at[18], "r3")
-    total = ((total + r3[...]).T * SCALE).astype(bf16)
+    total = ((total + r3[...].astype(f32)).T * SCALE).astype(bf16)
     for h in range(HEADS):
-        oq[:, h * HD:(h + 1) * HD] = total[h * ROWS:(h + 1) * ROWS, :]
+        oq[0, :, h * HD:(h + 1) * HD] = total[h * ROWS:(h + 1) * ROWS, :]
     for copy in started:
         copy.wait_send()
 
@@ -344,20 +343,18 @@
     vmem, smem, hbm = (pl.BlockSpec(memory_space=space) for space in (pltpu.VMEM, pltpu.SMEM, pltpu.HBM))
     dma = pltpu.SemaphoreType.DMA
     owned = KEYS // 8
-    grad_queries, grad_keys, grad_values = pl.pallas_call(
+    return pl.pallas_call(
         kernel,
         out_shape=(
-            jax.ShapeDtypeStruct((ROWS, HEADS * HD), bf16),
+            jax.ShapeDtypeStruct((1, ROWS, HEADS * HD), bf16),
             jax.ShapeDtypeStruct((owned, HD), bf16),
             jax.ShapeDtypeStruct((owned, HD), bf16),
         ),
-        in_specs=[hbm] * 6 + [smem] * 2,
+        in_specs=[hbm] * 2 + [vmem] * 2 + [hbm] * 2 + [smem] * 2,
         out_specs=(vmem, vmem, vmem),
         scratch_shapes=[
             pltpu.VMEM((ROWS, HEADS * HD), bf16),
             pltpu.VMEM((ROWS, HEADS * HD), bf16),
-            pltpu.VMEM((HEADS, ROWS), bf16),
-            pltpu.VMEM((HEADS, ROWS), bf16),
             pltpu.VMEM((KEYS, HD), bf16),
             pltpu.VMEM((KEYS, HD), bf16),
             pltpu.VMEM((2, 4, 4, DO + SLOT, HD), bf16),
@@ -370,20 +367,19 @@
             pltpu.VMEM((2, 3, 4, HD, SLOT), bf16),
             pltpu.VMEM((6, HD, SLOT), bf16),
             pltpu.VMEM((6, HD, SLOT), bf16),
-            pltpu.VMEM((HD, SLOT), f32),
-            pltpu.VMEM((HD, SLOT), f32),
+            pltpu.VMEM((HD, SLOT), bf16),
+            pltpu.VMEM((HD, SLOT), bf16),
             pltpu.VMEM((4, TILE, HD), bf16),
             pltpu.VMEM((4, TILE, HD), bf16),
             pltpu.VMEM((3 * TILE, HD), bf16),
             pltpu.VMEM((3 * TILE, HD), bf16),
-            dma((17,)), dma((25,)), dma((13,)), dma((6,)), dma((6,)),
+            dma((15,)), dma((25,)), dma((13,)), dma((6,)), dma((6,)),
             dma((19,)), dma((19,)), dma((4,)), dma((4,)), dma((7,)), dma((7,)),
             pltpu.SemaphoreType.REGULAR, pltpu.SemaphoreType.REGULAR,
         ],
         compiler_params=pltpu.CompilerParams(
             collective_id=0, has_side_effects=True, vmem_limit_bytes=64 * 1024 * 1024),
     )(queries[0], grad_out[0], row_lse[0].T, row_delta[0].T, prefix_keys, prefix_values, resp_len, visible)
-    return grad_queries[None], grad_keys, grad_values
 
 
 def solution(mesh):

time: 55.1 us -> 55.2 us (level)
  no operation moved by 1% of the time
where the time goes in v4:
time: 55.2 us; the launch traced here: 54.9 us
  Pallas kernels  50.1 us (91%)
  local copies, waits for them, and re-layouts  2.9 us (5%)
  between operations  1.94 us (4%)
    pallas_call x1, Pallas kernels, on_device(): pl.pallas_call(kernel, out_shape=(jax.ShapeDtypeStruct((1, ROWS, HEADS *...  50.1 us
    unnamed x7, local copies, waits for them, and re-layouts  2.9 us

profile of v4, /device:TPU:32, one launch (start us, length us, event | category | flops | bytes accessed | tf_op | source)
XLA Modules:
  0.0 54.9 jit_solution(3848368228036835534)
XLA Ops:
  1.9 50.1 %shard_map.103 = (bf16[1,16,1024]{2,1,0:T(8,128)(2,1)}, bf16[256,128]{1,0:T(8,128)(2,1)}, bf16[256,128]{1,0:T(8,128)(2,1)}) custom-call(bf16[16,1024]{1,0:T(8,128)(2,1)} %bitcast.8, bf16[16,1024]{1,0:T(8,128)(2,1)} %bitcast.9, bf16[8,16]{1,0:T(8,128)(2,1)} %bitcast.10, bf16[8,16]{1,0:T(8,128)(2,1)} %bitcast.11, bf16[2048,128]{1,0:T(8,128)(2,1)} %k_in.1, ...), custom_call_target="tpu_custom_call" | custom-call | tf_op jit(solution)/shard_map/pallas_call | solution.py:346
  52.0 0.0 copy-start.1
  52.0 1.4 %copy.16 = bf16[1,16,1024]{2,1,0:T(8,128)(2,1)} copy(bf16[1,16,1024]{2,1,0:T(8,128)(2,1)} %get-tuple-element.6) | data formatting | bytes 65536
  53.4 0.0 copy-done.1
  53.4 0.0 copy-start
  53.5 0.6 %copy.17 = bf16[256,128]{1,0:T(8,128)(2,1)} copy(bf16[256,128]{1,0:T(8,128)(2,1)S(1)} %copy-done.1) | data formatting | bytes 131072
  54.1 0.2 copy-done
  54.3 0.6 %copy.18 = bf16[256,128]{1,0:T(8,128)(2,1)} copy(bf16[256,128]{1,0:T(8,128)(2,1)S(1)} %copy-done) | data formatting | bytes 131072
Async XLA Ops:
  52.0 1.4 %copy-start.1 = (bf16[256,128]{1,0:T(8,128)(2,1)S(1)}, bf16[256,128]{1,0:T(8,128)(2,1)}, u32[]{:S(2)}) copy-start(bf16[256,128]{1,0:T(8,128)(2,1)} %get-tuple-element.7) | copy-start | bytes 196612
  53.4 0.9 %copy-start = (bf16[256,128]{1,0:T(8,128)(2,1)S(1)}, bf16[256,128]{1,0:T(8,128)(2,1)}, u32[]{:S(2)}) copy-start(bf16[256,128]{1,0:T(8,128)(2,1)} %get-tuple-element.8) | copy-start | bytes 196612
